TPU v7x, 32 devices: a whole 2x2x4 slice. The times are simulated.
32 devices in a mesh: seq: 8 (over y, x, core), dp: 4 (over z).
Axes of the slice: x: 2, y: 2, z: 4, core: 2. Of those that a mesh axis runs over, the one named last changes fastest.
Arguments:
- tokens: bfloat16 [4, 4096, 2048], P('dp', 'seq'), may hold values from -6 to 6
- weights_master: float32 [2048, 3072], P('dp'), may hold values from -0.125 to 0.125
- adam_first: float32 [2048, 3072], P('dp'), may hold values from -6 to 6
- adam_second: float32 [2048, 3072], P('dp'), may hold values from 0.5 to 2
- cotangent: bfloat16 [4, 4096, 1024], P('dp', 'seq'), may hold values from -0.046875 to 0.046875
Outputs:
- attended: bfloat16 [4, 4096, 1024], P('dp', 'seq')
- new_weights: float32 [2048, 3072], P('dp')
- new_first: float32 [2048, 3072], P('dp')
- new_second: float32 [2048, 3072], P('dp')
All inputs are finite; a program needn't handle non-finite values.
Results may differ from a plain program's by a relative error of at most 0.0035.
The roundings to bfloat16 on the way count: a program that leaves them out, or rounds other values in their place, can miss the bound.
Values may be sent and summed in bfloat16 or wider, within the bound.
A program may use at most 128 MiB of HBM per device.

v0:
```python
import jax
import jax.numpy as jnp
from jax import lax
from jax.sharding import PartitionSpec as P

HDIM = 128
BLOCK = 512
STEP = 100


EPS_NORM = 1e-05
BETA_ONE = 0.9
BETA_TWO = 0.95
LEARN_RATE = 0.001
DECAY_WEIGHT = 0.1
EPS_ADAM = 1e-08


def causal_table():
    places = jnp.arange(BLOCK, dtype=jnp.int32)
    return places[:, None] >= places[None, :]


def block_scores(query_block, key_block):
    causal = causal_table()
    scores = jnp.einsum("the,she->hts", query_block, key_block, preferred_element_type=jnp.float32)
    return jnp.where(causal[None], scores, 0.0).astype(jnp.bfloat16)


def forward_block(operands):
    query_block, key_block, value_block, carried_state = operands
    scores = block_scores(query_block, key_block)
    within = jnp.einsum("hts,she->the", scores, value_block, preferred_element_type=jnp.float32)
    carried = jnp.einsum(
        "the,hef->thf", query_block, carried_state, preferred_element_type=jnp.float32
    )
    return within + carried


def backward_block(operands):
    query_block, key_block, value_block, grad_block, carried_state, later_state = operands
    causal = causal_table()
    scores = block_scores(query_block, key_block)
    back = jnp.einsum("thf,shf->hts", grad_block, value_block, preferred_element_type=jnp.float32)
    back = jnp.where(causal[None], back, 0.0).astype(jnp.bfloat16)
    grad_query = jnp.einsum("hts,she->the", back, key_block, preferred_element_type=jnp.float32)
    grad_query = grad_query + jnp.einsum(
        "thf,hef->the", grad_block, carried_state, preferred_element_type=jnp.float32
    )
    grad_key = jnp.einsum("hts,the->she", back, query_block, preferred_element_type=jnp.float32)
    grad_key = grad_key + jnp.einsum(
        "shf,hef->she", value_block, later_state, preferred_element_type=jnp.float32
    )
    grad_value = jnp.einsum("hts,thf->shf", scores, grad_block, preferred_element_type=jnp.float32)
    grad_value = grad_value + jnp.einsum(
        "she,hef->shf", key_block, later_state, preferred_element_type=jnp.float32
    )
    block_rows = query_block.shape[0]
    joined = jnp.concatenate(
        [
            grad_query.reshape(block_rows, -1),
            grad_key.reshape(block_rows, -1),
            grad_value.reshape(block_rows, -1),
        ],
        axis=1,
    )
    return joined.astype(jnp.bfloat16)


def local(tokens, weights_master, adam_first, adam_second, cotangent):
    inputs = tokens[0]
    row_total = inputs.shape[0]
    model_dim = inputs.shape[1]
    inner_width = cotangent.shape[2]
    head_count = inner_width // HDIM
    blocks = row_total // BLOCK
    triple = 3 * inner_width
    position = lax.axis_index("seq")
    weights_bf = weights_master.astype(jnp.bfloat16)
    columns = inputs
    projected = jnp.dot(
        columns,
        lax.all_gather(weights_bf, "dp", axis=0, tiled=True),
        preferred_element_type=jnp.float32,
    )
    qkv = projected.astype(jnp.bfloat16)
    queries = qkv[:, :inner_width].reshape(blocks, BLOCK, head_count, HDIM)
    key_heads = qkv[:, inner_width : 2 * inner_width].reshape(blocks, BLOCK, head_count, HDIM)
    value_heads = qkv[:, 2 * inner_width :].reshape(blocks, BLOCK, head_count, HDIM)
    kv_local = jnp.einsum(
        "bshe,bshf->bhef", key_heads, value_heads, preferred_element_type=jnp.float32
    )
    kv_total = jnp.sum(kv_local, 0)
    state_zeros = jnp.zeros(kv_total.shape, jnp.float32)
    incoming = lax.all_gather(kv_total[None], "seq", axis=0, tiled=True)
    owners = jnp.arange(incoming.shape[0], dtype=jnp.int32)
    kept = jnp.where((owners < position)[:, None, None, None], incoming, 0.0)
    kv_before = jnp.sum(kept, 0)
    prefix_state = (kv_before[None] + (jnp.cumsum(kv_local, 0) - kv_local)).astype(jnp.bfloat16)
    mixed = lax.map(forward_block, (queries, key_heads, value_heads, prefix_state))
    inverse_rms = lax.rsqrt(jnp.mean(mixed * mixed, -1, keepdims=True) + EPS_NORM)
    normed = mixed * inverse_rms
    attended = normed.astype(jnp.bfloat16).reshape(1, row_total, inner_width)
    grad_out = cotangent[0].astype(jnp.float32).reshape(blocks, BLOCK, head_count, HDIM)
    along = jnp.mean(grad_out * normed, -1, keepdims=True)
    grad_mixed = (inverse_rms * (grad_out - normed * along)).astype(jnp.bfloat16)
    qg_local = jnp.einsum(
        "bthe,bthf->bhef", queries, grad_mixed, preferred_element_type=jnp.float32
    )
    qg_total = jnp.sum(qg_local, 0)
    incoming = lax.all_gather(
        qg_total[None].astype(jnp.bfloat16), "seq", axis=0, tiled=True
    ).astype(jnp.float32)
    owners = jnp.arange(incoming.shape[0], dtype=jnp.int32)
    kept = jnp.where((owners > position)[:, None, None, None], incoming, 0.0)
    qg_after = state_zeros + jnp.sum(kept, 0)
    suffix_state = (qg_after[None] + (jnp.cumsum(qg_local[::-1], 0)[::-1] - qg_local)).astype(
        jnp.bfloat16
    )
    grad_qkv = lax.map(
        backward_block, (queries, key_heads, value_heads, grad_mixed, prefix_state, suffix_state)
    )
    grad_qkv = grad_qkv.reshape(row_total, triple)
    seq_count = lax.axis_size("seq")
    dp_count = lax.axis_size("dp")
    piece_rows = model_dim // (seq_count * dp_count)
    reordered = inputs.reshape(row_total, dp_count, seq_count, piece_rows)
    reordered = jnp.transpose(reordered, (0, 2, 1, 3)).reshape(row_total, model_dim)
    columns = reordered
    partial_value = jnp.einsum(
        "td,tc->dc", columns, grad_qkv, preferred_element_type=jnp.float32
    ).astype(jnp.bfloat16)
    partial_value = lax.optimization_barrier(partial_value)
    summed = lax.psum_scatter(
        partial_value.astype(jnp.float32), ("seq", "dp"), scatter_dimension=0, tiled=True
    )
    gradient = lax.all_gather(summed.astype(jnp.bfloat16), "seq", axis=0, tiled=True).astype(
        summed.dtype
    )
    new_first = BETA_ONE * adam_first + (1.0 - BETA_ONE) * gradient
    new_second = BETA_TWO * adam_second + (1.0 - BETA_TWO) * gradient * gradient
    first_hat = new_first / (1.0 - BETA_ONE**STEP)
    second_hat = new_second / (1.0 - BETA_TWO**STEP)
    new_weights = weights_master - LEARN_RATE * (
        first_hat / (jnp.sqrt(second_hat) + EPS_ADAM) + DECAY_WEIGHT * weights_master
    )
    return (attended, new_weights, new_first, new_second)


def solution(mesh):
    placed = (
        P("dp", "seq", None),
        P("dp", None),
        P("dp", None),
        P("dp", None),
        P("dp", "seq", None),
    )
    return jax.shard_map(
        local,
        mesh=mesh,
        in_specs=placed,
        out_specs=(P("dp", "seq", None), P("dp", None), P("dp", None), P("dp", None)),
        check_vma=False,
    )
```

profile of v0, /device:TPU:9, one launch (start us, length us, event | category | flops | bytes accessed | tf_op | source)
XLA Modules:
  0.0 652.7 jit_solution(4909562181516776928)
XLA Ops:
  7.2 0.0 all-gather.7.cloned.1.call-start
  7.2 5.1 convert_element_type.69
  12.3 0.0 all-gather.11.cloned.1.call-start
  12.4 216.7 %all-gather.7.cloned.1.call-done = bf16[2048,3072]{1,0:T(8,128)(2,1)} async-done(((bf16[512,3072]{1,0:T(8,128)(2,1)}), bf16[2048,3072]{1,0:T(8,128)(2,1)}) %all-gather.7.cloned.1.call-update) | async-done | bytes 12582928 | tf_op jit(solution)/shard_map/all_gather | solution.py:83
  229.0 9.6 %convolution_convert_fusion = bf16[512,3072]{1,0:T(8,128)(2,1)S(1)} fusion(bf16[2048,3072]{1,0:T(8,128)(2,1)} %all-gather.7.cloned.1.call-done, bf16[1,512,2048]{2,1,0:T(8,128)(2,1)S(1)} %copy-done.14), kind=kOutput, calls=%fused_computation.8 | convolution fusion | flops 6444023808 | bytes 17825792 | tf_op jit(solution)/shard_map/dot_general | solution.py:81
  238.6 2.3 slice_bitcast_fusion.2
  240.9 0.3 copy.117
  241.2 0.7 copy.88
  241.9 1.3 fusion.17
  243.2 0.0 all-gather.13.cloned.1.call-start
  243.2 1.5 copy.92
  244.8 0.1 iota_compare_fusion
  244.9 2.4 copy.114
  247.3 2.9 select_convert_fusion.1
  250.2 2.0 copy-done
  252.2 2.9 fusion.13
  255.1 26.4 %all-gather.11.cloned.1.call-done = f32[64,128,128]{2,1,0:T(8,128)} async-done(((f32[8,128,128]{2,1,0:T(8,128)}), f32[64,128,128]{2,1,0:T(8,128)}) %all-gather.11.cloned.1.call-update) | async-done | bytes 4194320 | tf_op jit(solution)/shard_map/all_gather | solution.py:95
  281.5 2.9 select_reduce_fusion
  284.4 0.1 add_convert_fusion.4
  284.5 0.3 copy-done.10
  284.8 0.5 fusion.8
  285.4 0.6 multiply_reduce_fusion
  285.9 1.7 multiply_convert_fusion
  287.6 1.0 copy-done.2
  288.6 1.3 fusion.28
  289.9 0.2 reduce-scatter.4.cloned.1.call-start
  290.2 4.1 copy.103
  294.2 3.1 copy.104
  297.4 1.4 select_convert_fusion
  298.8 1.5 fusion.29
  300.3 1.4 add_convert_fusion.2
  301.7 2.0 fusion.31
  303.8 2.0 fusion.30
  305.8 12.1 %all-gather.13.cloned.1.call-done = bf16[64,128,128]{2,1,0:T(8,128)(2,1)} async-done(((bf16[8,128,128]{2,1,0:T(8,128)(2,1)}), bf16[64,128,128]{2,1,0:T(8,128)(2,1)}) %all-gather.13.cloned.1.call-update) | async-done | bytes 2097168 | tf_op jit(solution)/shard_map/all_gather | solution.py:111
  318.0 2.3 fusion.2
  320.3 1.1 add_convert_fusion.3
  321.4 0.5 add_convert_fusion
  322.0 0.5 add_convert_fusion.1
  322.4 0.5 copy-done.15
  323.0 0.3 copy-done.16
  323.3 9.9 %convert_bitcast_fusion = bf16[2048,3072]{0,1:T(8,128)(2,1)} fusion(bf16[512,2048]{0,1:T(8,128)(2,1)S(1)} %bitcast.87, bf16[512,1024]{0,1:T(8,128)(2,1)S(1)} %bitcast.90, bf16[512,1024]{0,1:T(8,128)(2,1)S(1)} %bitcast.91, bf16[512,1024]{0,1:T(8,128)(2,1)S(1)} %bitcast.89), kind=kOutput, calls=%fused_computation | convolution fusion | flops 6458179584 | bytes 17825792 | tf_op jit(solution)/shard_map/td,tc->dc/dot_general | solution.py:130
  333.2 17.9 %copy.112 = f32[2048,3072]{1,0:T(8,128)} copy(bf16[2048,3072]{0,1:T(8,128)(2,1)} %convert_bitcast_fusion) | data formatting | bytes 37748736
  351.1 0.3 all-gather.9.cloned.1.call-start
  351.4 244.8 %reduce-scatter.4.cloned.1.call-done = f32[64,3072]{1,0:T(8,128)} async-done(((f32[2048,3072]{1,0:T(8,128)}), f32[64,3072]{1,0:T(8,128)}) %reduce-scatter.4.cloned.1.call-update) | async-done | bytes 786448 | tf_op jit(solution)/shard_map/reduce_scatter | solution.py:134
  596.1 1.9 convert_element_type.85
  598.1 1.3 copy.106
  599.4 31.7 %all-gather.9.cloned.1.call-done = bf16[512,3072]{1,0:T(8,128)(2,1)} async-done(((bf16[64,3072]{1,0:T(8,128)(2,1)}), bf16[512,3072]{1,0:T(8,128)(2,1)}) %all-gather.9.cloned.1.call-update) | async-done | bytes 3145744 | tf_op jit(solution)/shard_map/all_gather | solution.py:137
  631.1 15.0 %multiply_subtract_fusion = (f32[512,3072]{1,0:T(8,128)}, f32[512,3072]{1,0:T(8,128)}, f32[512,3072]{1,0:T(8,128)}) fusion(f32[512,3072]{1,0:T(8,128)} %param.6, bf16[512,3072]{1,0:T(8,128)(2,1)} %all-gather.9.cloned.1.call-done, f32[512,3072]{1,0:T(8,128)} %param.7, f32[512,3072]{1,0:T(8,128)} %param.8), kind=kLoop, calls=%fused_computation.7 | loop fusion | flops 25165824 | bytes 40894464 | tf_op jit(solution)/shard_map/sub | solution.py:144
  (42 shorter events, 0.2 us)
Async XLA Ops:
  7.2 221.8 %copy-start.14 = (bf16[1,512,2048]{2,1,0:T(8,128)(2,1)S(1)}, bf16[1,512,2048]{2,1,0:T(8,128)(2,1)}, u32[]{:S(2)}) copy-start(bf16[1,512,2048]{2,1,0:T(8,128)(2,1)} %param.5) | copy-start | bytes 6291460
  7.2 221.8 %all-gather.7.cloned.1.call-start = ((), (), s32[]{:S(2)}) async-start(), calls=%async_computation.1 | async-start | bytes 15728640 | tf_op jit(solution)/shard_map/all_gather | solution.py:83
  12.3 269.2 %all-gather.11.cloned.1.call-start = ((), (), s32[]{:S(2)}) async-start(), calls=%async_computation.3 | async-start | bytes 4718592 | tf_op jit(solution)/shard_map/all_gather | solution.py:95
  241.9 1.3 copy-start.6
  243.2 74.8 %all-gather.13.cloned.1.call-start = ((), (), s32[]{:S(2)}) async-start(), calls=%async_computation.4 | async-start | bytes 2359296 | tf_op jit(solution)/shard_map/all_gather | solution.py:111
  244.8 5.4 copy-start.17
  250.2 2.0 copy-start
  281.5 2.9 copy-start.11
  281.5 3.0 copy-start.4
  281.5 3.3 copy-start.10
  287.6 1.0 copy-start.2
  289.9 7.4 %copy-start.3 = (bf16[512,8,128]{0,2,1:T(8,128)(2,1)S(1)}, bf16[512,8,128]{0,2,1:T(8,128)(2,1)}, u32[]{:S(2)}) copy-start(bf16[512,8,128]{0,2,1:T(8,128)(2,1)} %copy-done.2) | copy-start | bytes 3145732
  289.9 7.4 %copy-start.18 = (pred[512,512]{1,0:T(8,128)(4,1)S(1)}, pred[512,512]{1,0:T(8,128)(4,1)}, u32[]{:S(2)}) copy-start(pred[512,512]{1,0:T(8,128)(4,1)} %copy-done.17) | copy-start | bytes 786436
  289.9 306.2 %reduce-scatter.4.cloned.1.call-start = ((), (), s32[]{:S(2)}) async-start(), calls=%async_computation.5 | async-start | bytes 25952256 | tf_op jit(solution)/shard_map/reduce_scatter | solution.py:134
  297.4 1.4 copy-start.7
  298.8 2.9 copy-start.1
  301.7 2.0 copy-start.5
  303.8 17.6 %copy-start.8 = (f32[8,128,512]{2,1,0:T(8,128)S(1)}, f32[8,128,512]{2,1,0:T(8,128)}, u32[]{:S(2)}) copy-start(f32[8,128,512]{2,1,0:T(8,128)} %fusion.31) | copy-start | bytes 6291460
  318.0 3.4 copy-start.12
  318.0 4.0 copy-start.9
  321.4 1.6 copy-start.15
  321.4 1.8 copy-start.16
  351.1 247.0 %copy-start.13 = (bf16[512,8,128]{0,2,1:T(8,128)(2,1)S(1)}, bf16[512,8,128]{0,2,1:T(8,128)(2,1)}, u32[]{:S(2)}) copy-start(bf16[512,8,128]{0,2,1:T(8,128)(2,1)} %get-tuple-element.70) | copy-start | bytes 3145732
  351.1 280.0 %all-gather.9.cloned.1.call-start = ((), (), s32[]{:S(2)}) async-start(), calls=%async_computation.2 | async-start | bytes 3538944 | tf_op jit(solution)/shard_map/all_gather | solution.py:137
Sparse Core Ops, SparseCore 0:
  12.4 216.5 all-gather.6
  243.3 38.1 all-gather.10
  290.0 27.8 all-gather.12
  351.2 244.8 reduce-scatter.3
  598.6 32.4 all-gather.8
where the time goes:
time: 655 us; the launch traced here: 653 us
  waiting for transfers between devices  532 us (81%)
  matrix products  37.9 us (6%)
  local copies, waits for them, and re-layouts  37.7 us (6%)
  other arithmetic  30.7 us (5%)
  between operations  14.1 us (2%)
    reduce_scatter x1, waiting for transfers between devices, local(): lax.psum_scatter(partial_value.astype(jnp.float32), ('seq', 'dp'), scatte...  245 us
    all_gather x1, waiting for transfers between devices, local(): lax.all_gather(weights_bf, 'dp', axis=0, tiled=True)  217 us
    all_gather x1, waiting for transfers between devices, local(): lax.all_gather(summed.astype(jnp.bfloat16), 'seq', axis=0, tiled=True)  31.7 us
    unnamed x43, local copies, waits for them, and re-layouts  30 us
    all_gather x1, waiting for transfers between devices, local(): incoming = lax.all_gather(kv_total[None], 'seq', axis=0, tiled=True)  26.4 us
    sub x1, other arithmetic, local(): weights_master - LEARN_RATE * (first_hat / (jnp.sqrt(second_hat) + EPS_AD...  15 us
  transfers between devices with their start and end apart: 5, of which 5 were waited for; matrix products, arithmetic and copies ran while one was open for 4% of the time, Pallas kernels for 0%

commit v1 on v0

--- a/solution.py
+++ b/solution.py
@@ -1,6 +1,10 @@
+import functools
+
 import jax
 import jax.numpy as jnp
 from jax import lax
+from jax.experimental import pallas as pl
+from jax.experimental.pallas import tpu as pltpu
 from jax.sharding import PartitionSpec as P
 
 HDIM = 128
@@ -67,7 +71,18 @@
     return joined.astype(jnp.bfloat16)
 
 
-def local(tokens, weights_master, adam_first, adam_second, cotangent):
+def adam_step(weights_master, adam_first, adam_second, gradient):
+    new_first = BETA_ONE * adam_first + (1.0 - BETA_ONE) * gradient
+    new_second = BETA_TWO * adam_second + (1.0 - BETA_TWO) * gradient * gradient
+    first_hat = new_first / (1.0 - BETA_ONE**STEP)
+    second_hat = new_second / (1.0 - BETA_TWO**STEP)
+    new_weights = weights_master - LEARN_RATE * (
+        first_hat / (jnp.sqrt(second_hat) + EPS_ADAM) + DECAY_WEIGHT * weights_master
+    )
+    return new_weights, new_first, new_second
+
+
+def token_split(tokens, weights_master, adam_first, adam_second, cotangent):
     inputs = tokens[0]
     row_total = inputs.shape[0]
     model_dim = inputs.shape[1]
@@ -137,14 +152,424 @@
     gradient = lax.all_gather(summed.astype(jnp.bfloat16), "seq", axis=0, tiled=True).astype(
         summed.dtype
     )
-    new_first = BETA_ONE * adam_first + (1.0 - BETA_ONE) * gradient
-    new_second = BETA_TWO * adam_second + (1.0 - BETA_TWO) * gradient * gradient
-    first_hat = new_first / (1.0 - BETA_ONE**STEP)
-    second_hat = new_second / (1.0 - BETA_TWO**STEP)
-    new_weights = weights_master - LEARN_RATE * (
-        first_hat / (jnp.sqrt(second_hat) + EPS_ADAM) + DECAY_WEIGHT * weights_master
-    )
-    return (attended, new_weights, new_first, new_second)
+    return (attended,) + adam_step(weights_master, adam_first, adam_second, gradient)
+
+
+CHUNKS = 4
+
+
+def mm(left, right, dims):
+    return lax.dot_general(left, right, (dims, ((), ())), preferred_element_type=jnp.float32)
+
+
+NN = ((1,), (0,))
+NT = ((1,), (1,))
+TN = ((0,), (0,))
+
+
+def head_kernel(
+    dp_count,
+    tokens_ref,
+    weights_ref,
+    cot_ref,
+    att_out,
+    grad_out,
+    tok,
+    w_stage,
+    w_bf,
+    cot,
+    qkv,
+    scores,
+    prefix,
+    att,
+    grad_mixed,
+    grad_t,
+    part,
+    part_in,
+    total,
+    gathered,
+    state,
+    local_sem,
+    tok_recv,
+    tok_send,
+    relay_send,
+    twin_send,
+    w_recv,
+    w_send,
+    cot_recv,
+    cot_send,
+    att_recv,
+    att_send,
+    part_recv,
+    part_send,
+    sum_recv,
+    sum_send,
+):
+    me = lax.axis_index("seq")
+    row = lax.axis_index("dp")
+    depth = weights_ref.shape[0]
+    heads = 8
+    inner = heads * HDIM
+    width = 3 * HDIM
+    side = 1 - 2 * (me % 2)
+    step_x = 2 - 4 * ((me // 2) % 2)
+    step_y = 4 - 8 * (me // 4)
+    twin = me + side
+    near_x = me + step_x
+    near_y = me + step_y
+    far = me + step_x + step_y
+    others = [
+        me + step_x + step_y + side,
+        far,
+        near_x + side,
+        near_y + side,
+        near_x,
+        near_y,
+        twin,
+    ]
+    size = BLOCK // CHUNKS
+
+    def block(index):
+        return pl.ds(pl.multiple_of(index * BLOCK, BLOCK), BLOCK)
+
+    def piece(index, chunk):
+        return pl.ds(pl.multiple_of(index * BLOCK + chunk * size, size), size)
+
+    def head_cols(index, part_index):
+        return pl.ds(pl.multiple_of(part_index * inner + index * HDIM, HDIM), HDIM)
+
+    def remote(src, dst, send, recv, **axis):
+        return pltpu.make_async_remote_copy(
+            src_ref=src,
+            dst_ref=dst,
+            send_sem=send,
+            recv_sem=recv,
+            device_id=axis,
+            device_id_type=pl.DeviceIdType.MESH,
+        )
+
+    fetch = [
+        pltpu.make_async_copy(
+            weights_ref.at[:, head_cols(me, i)],
+            w_stage.at[:, pl.ds(i * HDIM, HDIM)],
+            local_sem.at[i],
+        )
+        for i in range(3)
+    ]
+    for copy in fetch:
+        copy.start()
+    own_tok = pltpu.make_async_copy(tokens_ref, tok.at[block(me), :], local_sem.at[3])
+    own_tok.start()
+    own_cot = pltpu.make_async_copy(
+        cot_ref.at[:, head_cols(me, 0)], cot.at[block(me), :], local_sem.at[4]
+    )
+    own_cot.start()
+
+    barrier = pltpu.get_barrier_semaphore()
+    for other in others:
+        pl.semaphore_signal(
+            barrier, inc=1, device_id={"seq": other}, device_id_type=pl.DeviceIdType.MESH
+        )
+    for r in range(1, dp_count):
+        pl.semaphore_signal(
+            barrier,
+            inc=1,
+            device_id={"dp": (row + r) % dp_count},
+            device_id_type=pl.DeviceIdType.MESH,
+        )
+    pl.semaphore_wait(barrier, len(others) + dp_count - 1)
+
+    waits = []
+
+    def send(copy):
+        copy.start()
+        waits.append(copy)
+
+    def own_piece(chunk, slot, target):
+        send(
+            remote(
+                tokens_ref.at[pl.ds(chunk * size, size), :],
+                tok.at[piece(me, chunk), :],
+                tok_send.at[slot, chunk],
+                tok_recv.at[me, chunk],
+                seq=target,
+            )
+        )
+
+    x_order = [0, 1, 2, 3]
+    y_order = [2, 3, 0, 1]
+    for t in range(CHUNKS):
+        own_piece(x_order[t], 0, near_x)
+        own_piece(y_order[t], 1, near_y)
+    for t in range(CHUNKS):
+        own_piece(t, 2, twin)
+
+    for copy in fetch:
+        copy.wait()
+    own_rows = pl.ds(pl.multiple_of(row * depth, depth), depth)
+    w_bf[own_rows, :] = w_stage[...].astype(jnp.bfloat16)
+    for r in range(1, dp_count):
+        send(
+            remote(
+                w_bf.at[own_rows, :],
+                w_bf.at[own_rows, :],
+                w_send.at[r],
+                w_recv.at[row],
+                dp=(row + r) % dp_count,
+            )
+        )
+
+    def arrived(source, chunk):
+        place = tok.at[piece(source, chunk), :]
+        remote(place, place, tok_send.at[0, 0], tok_recv.at[source, chunk], seq=twin).wait_recv()
+
+    def pass_on(source, chunk, send_sem, target):
+        place = tok.at[piece(source, chunk), :]
+        send(remote(place, place, send_sem, tok_recv.at[source, chunk], seq=target))
+
+    def project(source):
+        qkv[block(source), :] = mm(tok[block(source), :], w_bf[...], NN).astype(jnp.bfloat16)
+
+    for t in range(CHUNKS):
+        arrived(near_x, x_order[t])
+        if t < CHUNKS // 2:
+            pass_on(near_x, x_order[t], relay_send.at[0, t], near_y)
+        arrived(near_y, y_order[t])
+        if t < CHUNKS // 2:
+            pass_on(near_y, y_order[t], relay_send.at[1, t], near_x)
+        pass_on(near_x, x_order[t], twin_send.at[0, t], twin)
+        pass_on(near_y, y_order[t], twin_send.at[1, t], twin)
+    for r in range(1, dp_count):
+        source = (row + dp_count - r) % dp_count
+        rows = w_bf.at[pl.ds(pl.multiple_of(source * depth, depth), depth), :]
+        remote(rows, rows, w_send.at[r], w_recv.at[source], dp=source).wait_recv()
+    own_tok.wait()
+    for t in range(CHUNKS):
+        arrived(twin, t)
+    project(me)
+    project(twin)
+    for t in range(CHUNKS // 2):
+        arrived(far, x_order[t])
+        arrived(far, y_order[t])
+        pass_on(far, x_order[t], twin_send.at[2, 2 * t], twin)
+        pass_on(far, y_order[t], twin_send.at[2, 2 * t + 1], twin)
+        if t == 0:
+            for k, other in enumerate(others):
+                send(
+                    remote(
+                        cot_ref.at[:, head_cols(other, 0)],
+                        cot.at[block(me), :],
+                        cot_send.at[k],
+                        cot_recv.at[me],
+                        seq=other,
+                    )
+                )
+            project(near_x)
+            project(near_y)
+            for source in (near_x + side, near_y + side):
+                for chunk in range(CHUNKS):
+                    arrived(source, chunk)
+                project(source)
+    project(far)
+    for chunk in range(CHUNKS):
+        arrived(far + side, chunk)
+    project(far + side)
+    own_cot.wait()
+    for other in others:
+        place = cot.at[block(other), :]
+        remote(place, place, cot_send.at[0], cot_recv.at[other], seq=other).wait_recv()
+
+    causal = lax.broadcasted_iota(jnp.int32, (BLOCK, BLOCK), 0) >= lax.broadcasted_iota(
+        jnp.int32, (BLOCK, BLOCK), 1
+    )
+    state[...] = jnp.zeros_like(state)
+
+    def forward(b, carry):
+        rows = block(b)
+        query = qkv[rows, 0:HDIM]
+        key = qkv[rows, HDIM : 2 * HDIM]
+        value = qkv[rows, 2 * HDIM : width]
+        before = state[...].astype(jnp.bfloat16)
+        prefix[b] = before
+        table = jnp.where(causal, mm(query, key, NT), 0.0).astype(jnp.bfloat16)
+        scores[rows, :] = table
+        mixed = mm(table, value, NN) + mm(query, before, NN)
+        inverse_rms = lax.rsqrt(jnp.mean(mixed * mixed, -1, keepdims=True) + EPS_NORM)
+        normed = mixed * inverse_rms
+        att[rows, :] = normed.astype(jnp.bfloat16)
+        given = cot[rows, :].astype(jnp.float32)
+        along = jnp.mean(given * normed, -1, keepdims=True)
+        grad_mixed[rows, :] = (inverse_rms * (given - normed * along)).astype(jnp.bfloat16)
+        state[...] += mm(key, value, TN)
+        return carry
+
+    lax.fori_loop(0, heads, forward, 0)
+
+    own_att = pltpu.make_async_copy(
+        att.at[block(me), :], att_out.at[:, head_cols(me, 0)], local_sem.at[5]
+    )
+    own_att.start()
+    for k, other in enumerate(others):
+        send(
+            remote(
+                att.at[block(other), :],
+                att_out.at[:, head_cols(me, 0)],
+                att_send.at[k],
+                att_recv.at[me],
+                seq=other,
+            )
+        )
+
+    state[...] = jnp.zeros_like(state)
+
+    def backward(step, carry):
+        rows = block(heads - 1 - step)
+        query = qkv[rows, 0:HDIM]
+        key = qkv[rows, HDIM : 2 * HDIM]
+        value = qkv[rows, 2 * HDIM : width]
+        grad = grad_mixed[rows, :]
+        later = state[...].astype(jnp.bfloat16)
+        before = prefix[heads - 1 - step]
+        table = scores[rows, :]
+        back = jnp.where(causal, mm(grad, value, NT), 0.0).astype(jnp.bfloat16)
+        grad_query = mm(back, key, NN) + mm(grad, before, NT)
+        grad_key = mm(back, query, TN) + mm(value, later, NT)
+        grad_value = mm(table, grad, TN) + mm(key, later, NN)
+        grad_t[0:HDIM, rows] = grad_query.T.astype(jnp.bfloat16)
+        grad_t[HDIM : 2 * HDIM, rows] = grad_key.T.astype(jnp.bfloat16)
+        grad_t[2 * HDIM : width, rows] = grad_value.T.astype(jnp.bfloat16)
+        state[...] += mm(query, grad, TN)
+        return carry
+
+    lax.fori_loop(0, heads, backward, 0)
+
+    def partial_sum(target):
+        columns = pl.ds(pl.multiple_of(target * depth, depth), depth)
+        gathered[...] = jnp.zeros_like(gathered)
+
+        def add_block(b, carry):
+            rows = block(b)
+            share = mm(grad_t[:, rows], tok[rows, columns], NN)
+            gathered[...] += share.astype(jnp.bfloat16).astype(jnp.float32)
+            return carry
+
+        lax.fori_loop(0, heads, add_block, 0)
+        return gathered[...]
+
+    for r in range(1, dp_count):
+        target = (row + r) % dp_count
+        part[r] = partial_sum(target).astype(jnp.bfloat16)
+        send(remote(part.at[r], part_in.at[row], part_send.at[r], part_recv.at[row], dp=target))
+    summed = partial_sum(row)
+    for r in range(1, dp_count):
+        source = (row + dp_count - r) % dp_count
+        place = part_in.at[source]
+        remote(place, place, part_send.at[r], part_recv.at[source], dp=source).wait_recv()
+        summed = summed + part_in[source].astype(jnp.float32)
+    total[...] = summed.T
+
+    own_sum = []
+    for i in range(3):
+        piece_cols = total.at[:, pl.ds(i * HDIM, HDIM)]
+        for k, other in enumerate((near_x, near_y, far, twin)):
+            send(
+                remote(
+                    piece_cols,
+                    grad_out.at[:, head_cols(me, i)],
+                    sum_send.at[k, i],
+                    sum_recv.at[me, i],
+                    seq=other,
+                )
+            )
+        own_sum.append(
+            pltpu.make_async_copy(
+                piece_cols, grad_out.at[:, head_cols(me, i)], local_sem.at[6 + i]
+            )
+        )
+        own_sum[i].start()
+
+    def sum_arrived(source, i):
+        place = grad_out.at[:, head_cols(source, i)]
+        remote(place, place, sum_send.at[0, 0], sum_recv.at[source, i], seq=twin).wait_recv()
+
+    for k, source in enumerate((near_x, near_y, far)):
+        for i in range(3):
+            sum_arrived(source, i)
+            place = grad_out.at[:, head_cols(source, i)]
+            send(remote(place, place, sum_send.at[4 + k, i], sum_recv.at[source, i], seq=twin))
+    for source in (twin, near_x + side, near_y + side, far + side):
+        for i in range(3):
+            sum_arrived(source, i)
+    for other in others:
+        place = att_out.at[:, head_cols(other, 0)]
+        remote(place, place, att_send.at[0], att_recv.at[other], seq=other).wait_recv()
+    own_att.wait()
+    for copy in own_sum:
+        copy.wait()
+    for copy in waits:
+        copy.wait_send()
+
+
+def head_split(tokens, weights_master, adam_first, adam_second, cotangent):
+    inputs = tokens[0]
+    model_dim = inputs.shape[1]
+    depth = weights_master.shape[0]
+    seq_count = lax.axis_size("seq")
+    dp_count = lax.axis_size("dp")
+    total_rows = seq_count * BLOCK
+    width = 3 * HDIM
+    anywhere = pl.BlockSpec(memory_space=pl.ANY)
+    dma = pltpu.SemaphoreType.DMA
+    attended, gradient = pl.pallas_call(
+        functools.partial(head_kernel, dp_count),
+        out_shape=(
+            jax.ShapeDtypeStruct((BLOCK, cotangent.shape[2]), jnp.bfloat16),
+            jax.ShapeDtypeStruct(weights_master.shape, jnp.float32),
+        ),
+        in_specs=[anywhere] * 3,
+        out_specs=(anywhere, anywhere),
+        scratch_shapes=[
+            pltpu.VMEM((total_rows, model_dim), jnp.bfloat16),
+            pltpu.VMEM((depth, width), jnp.float32),
+            pltpu.VMEM((model_dim, width), jnp.bfloat16),
+            pltpu.VMEM((total_rows, HDIM), jnp.bfloat16),
+            pltpu.VMEM((total_rows, width), jnp.bfloat16),
+            pltpu.VMEM((total_rows, BLOCK), jnp.bfloat16),
+            pltpu.VMEM((seq_count, HDIM, HDIM), jnp.bfloat16),
+            pltpu.VMEM((total_rows, HDIM), jnp.bfloat16),
+            pltpu.VMEM((total_rows, HDIM), jnp.bfloat16),
+            pltpu.VMEM((width, total_rows), jnp.bfloat16),
+            pltpu.VMEM((dp_count, width, depth), jnp.bfloat16),
+            pltpu.VMEM((dp_count, width, depth), jnp.bfloat16),
+            pltpu.VMEM((depth, width), jnp.float32),
+            pltpu.VMEM((width, depth), jnp.float32),
+            pltpu.VMEM((HDIM, HDIM), jnp.float32),
+            dma((9,)),
+            dma((seq_count, CHUNKS)),
+            dma((3, CHUNKS)),
+            dma((2, CHUNKS // 2)),
+            dma((3, CHUNKS)),
+            dma((dp_count,)),
+            dma((dp_count,)),
+            dma((seq_count,)),
+            dma((seq_count,)),
+            dma((seq_count,)),
+            dma((seq_count,)),
+            dma((dp_count,)),
+            dma((dp_count,)),
+            dma((seq_count, 3)),
+            dma((7, 3)),
+        ],
+        compiler_params=pltpu.CompilerParams(
+            collective_id=0, has_side_effects=True, vmem_limit_bytes=56 * 1024 * 1024
+        ),
+        cost_estimate=pl.CostEstimate(
+            flops=18 * 10**9, bytes_accessed=64 * 2**20, transcendentals=0
+        ),
+    )(inputs, weights_master, cotangent[0])
+    return (attended[None],) + adam_step(
+        weights_master, adam_first, adam_second, gradient
+    )
 
 
 def solution(mesh):
@@ -155,6 +580,13 @@
         P("dp", None),
         P("dp", "seq", None),
     )
+
+    def local(tokens, weights_master, adam_first, adam_second, cotangent):
+        heads = cotangent.shape[2] // HDIM
+        one_head_each = mesh.shape["seq"] == heads == 8 and tokens.shape[1] == BLOCK
+        form = head_split if one_head_each else token_split
+        return form(tokens, weights_master, adam_first, adam_second, cotangent)
+
     return jax.shard_map(
         local,
         mesh=mesh,

time: 655 us -> 191 us (0.29)
  waiting for transfers between devices: 532 us -> 0 us
  Pallas kernels: 0 us -> 176 us
  matrix products: 37.9 us -> 0 us
  local copies, waits for them, and re-layouts: 37.7 us -> 0.98 us
  other arithmetic: 30.7 us -> 13.4 us
  between operations: 14.1 us -> 0.66 us
    all_gather x4 -> x0, waiting for transfers between devices: 287 us -> none  [the longest x1 217 us: local(): lax.all_gather(weights_bf, 'dp', axis=0, tiled=True)]
    reduce_scatter x1 -> x0, waiting for transfers between devices: 245 us -> none  [local(): lax.psum_scatter(partial_value.astype(jnp.float32), ('seq', 'dp'), scatte...]
    pallas_call x0 -> x1, Pallas kernels: none -> 176 us  [head_split(): pl.pallas_call(functools.partial(head_kernel, dp_count), out_shape=(jax.S...]
    dot_general x14 -> x0, matrix products: 37.9 us -> none  [the longest x1 9.95 us: local(): jnp.einsum('td,tc->dc', columns, grad_qkv, preferred_element_type=jnp.flo...]
    unnamed x43 -> x5, local copies, waits for them, and re-layouts: 30 us -> 0.98 us
    convert_element_type x5 -> x0, other arithmetic: 9.8 us -> none  [the longest x1 5.06 us: local(): weights_bf = weights_master.astype(jnp.bfloat16)]
  transfers between devices with their start and end apart: 5 -> 0, of which waited for: 5 -> 0; matrix products, arithmetic and copies ran while one was open for 4% -> 0% of each run, Pallas kernels for 0% -> 0%
where the time goes in v1:
time: 191 us
  Pallas kernels  176 us (92%)
  other arithmetic  13.4 us (7%)
    pallas_call x1, Pallas kernels, head_split(): pl.pallas_call(functools.partial(head_kernel, dp_count), out_shape=(jax.S...  176 us
    sub x1, other arithmetic, adam_step(): weights_master - LEARN_RATE * (first_hat / (jnp.sqrt(second_hat) + EPS_AD...  13.4 us

profile of v1, /device:TPU:9, one launch (start us, length us, event | category | flops | bytes accessed | tf_op | source)
XLA Modules:
  0.0 191.1 jit_solution(14180579844048506378)
XLA Ops:
  0.6 0.0 copy-start
  0.6 176.0 %shard_map.84 = (bf16[512,1024]{1,0:T(8,128)(2,1)}, f32[512,3072]{1,0:T(8,128)}) custom-call(bf16[512,2048]{1,0:T(8,128)(2,1)} %bitcast.4, f32[512,3072]{1,0:T(8,128)} %weights_ref.1, bf16[512,1024]{1,0:T(8,128)(2,1)} %bitcast.5), custom_call_target="tpu_custom_call" | custom-call | flops 17999998976 | bytes 67108864 | tf_op jit(solution)/shard_map/pallas_call | solution.py:523
  176.7 0.0 copy-done
  176.7 0.0 copy-start.1
  176.7 13.4 %multiply_subtract_fusion = (f32[512,3072]{1,0:T(8,128)}, f32[512,3072]{1,0:T(8,128)}, f32[512,3072]{1,0:T(8,128)}) fusion(f32[512,3072]{1,0:T(8,128)S(1)} %copy-done, f32[512,3072]{1,0:T(8,128)} %get-tuple-element.7, f32[512,3072]{1,0:T(8,128)} %param.7, f32[512,3072]{1,0:T(8,128)} %param.8), kind=kLoop, calls=%fused_computation.2 | loop fusion | flops 23592960 | bytes 44040192 | tf_op jit(solution)/shard_map/sub | solution.py:79
  190.1 0.0 copy-done.1
  190.1 1.0 copy.10
Async XLA Ops:
  0.6 176.1 %copy-start = (f32[512,3072]{1,0:T(8,128)S(1)}, f32[512,3072]{1,0:T(8,128)}, u32[]{:S(2)}) copy-start(f32[512,3072]{1,0:T(8,128)} %weights_ref.1) | copy-start | bytes 18874372
  176.7 13.4 %copy-start.1 = (bf16[512,1024]{1,0:T(8,128)(2,1)S(1)}, bf16[512,1024]{1,0:T(8,128)(2,1)}, u32[]{:S(2)}) copy-start(bf16[512,1024]{1,0:T(8,128)(2,1)} %get-tuple-element.6) | copy-start | bytes 3145732
